TPU v7x, 256 devices: a whole 4x4x8 slice. The times are simulated.
256 devices in a mesh: row: 32 (over y_hi, z, core), rep: 8 (over y_lo, x).
Axes of the slice: x: 4, y: 4 (y_hi: 2, y_lo: 2; y = y_hi * 2 + y_lo), z: 8, core: 2. Of those that a mesh axis runs over, the one named last changes fastest.
Arguments:
- features: bfloat16 [24576, 256], P('row'), may hold values from -7 to 7
- adjacency: bfloat16 [24576, 24576], P('row', 'rep'), may hold values from -0.078125 to 0.078125
- tile_live: int32 [32, 32], P('row', 'rep'), may hold values from 0 to 1, as said below
- w_self: bfloat16 [256, 256], replicated, may hold values from -1.25 to 1.25
- w_neigh: bfloat16 [256, 256], replicated, may hold values from -1.25 to 1.25
- bias_vector: float32 [256], replicated, may hold values from -3 to 3
- pos_pairs: int32 [32, 1024, 3], P('row', 'rep'), may hold values from 0 to 640, as said below
- neg_pairs: int32 [32, 1024, 3], P('row', 'rep'), may hold values from 0 to 640, as said below
Outputs:
- embedding: bfloat16 [24576, 256], P(('row', 'rep'))
- pos_loss: float32 [32, 1024, 128], P('row', 'rep')
- neg_loss: float32 [32, 1024, 128], P('row', 'rep')
Inputs may be any that keep to these rules, and one draw needn't show every extreme that they name: `tile_live`: 1 marks a tile that counts (the adjacency holds nonzero values in every tile, live or not); every diagonal tile is live. `pos_pairs`: column 0 is below 6, column 1 below 4, column 2 at most 640, which is reached. `neg_pairs`: column 0 is below 6, column 1 below 4, column 2 at most 640, which is reached.
All inputs are finite; a program needn't handle non-finite values.
Results may differ from a plain program's by a relative error of at most 0.0037.
Values may be sent and summed in bfloat16 or wider, within the bound.
A program may use at most 128 MiB of HBM per device.

v0:
```python
import math

import jax
import jax.numpy as jnp
from jax import lax
from jax.sharding import PartitionSpec as P

PAIR_ROWS = 128


def from_root(block, axis, holder):
    block = jnp.where(lax.axis_index(axis) == holder, block, jnp.zeros_like(block))
    return lax.psum(block, axis)


def project_rows(own_feats, summed, w_self, w_neigh, bias_vector):
    projected = jnp.dot(own_feats, w_self, preferred_element_type=jnp.float32)
    projected = projected + jnp.dot(
        summed.astype(jnp.bfloat16), w_neigh, preferred_element_type=jnp.float32
    )
    projected = projected + bias_vector
    scaled = projected * lax.rsqrt(jnp.mean(projected * projected, axis=-1, keepdims=True) + 1e-06)
    return scaled.astype(jnp.bfloat16)


def pair_losses(pairs, direction, embedding_block, key_stack):
    blocksize, channels = embedding_block.shape
    query_tiles = embedding_block.reshape(blocksize // PAIR_ROWS, PAIR_ROWS, channels)
    queries = query_tiles[pairs[:, 0]]
    zero_index = jnp.zeros((), jnp.int32)

    def take_keys(section_id, offset):
        return lax.dynamic_slice(
            key_stack, (section_id, offset, zero_index), (1, PAIR_ROWS, channels)
        )[0]

    key_rows = jax.vmap(take_keys)(pairs[:, 1], pairs[:, 2])
    scores = jnp.einsum(
        "pqf,pkf->pqk", queries, key_rows, preferred_element_type=jnp.float32
    ) / math.sqrt(channels)
    return jnp.mean(jax.nn.softplus(direction * scores), axis=-1)


def per_device(features, adjacency, tile_live, w_self, w_neigh, bias_vector, pos_pairs, neg_pairs):
    blocksize = features.shape[0]
    channels = features.shape[1]
    sections = tile_live.shape[1]
    replica = lax.axis_index("rep")
    first_section = replica * sections
    live_flags = tile_live[0]
    sources = [from_root(features, "row", first_section + section) for section in range(sections)]
    running = jnp.zeros((blocksize, channels), jnp.float32)
    for section in range(sections):
        tile_now = adjacency[:, section * blocksize : (section + 1) * blocksize]
        source_now = sources[section]
        product = jnp.dot(tile_now, source_now, preferred_element_type=jnp.float32)
        running = running + jnp.where(live_flags[section] > 0, product, 0.0)
    share = lax.psum_scatter(running, "rep", scatter_dimension=0, tiled=True)
    own_feats = lax.dynamic_slice_in_dim(features, replica * share.shape[0], share.shape[0], 0)
    embedding = project_rows(own_feats, share, w_self, w_neigh, bias_vector)
    embedding_block = lax.all_gather(embedding, "rep", axis=0, tiled=True)
    key_stack = jnp.stack(
        [from_root(embedding_block, "row", first_section + section) for section in range(sections)]
    )
    pos_loss = pair_losses(pos_pairs[0], -1.0, embedding_block, key_stack)
    neg_loss = pair_losses(neg_pairs[0], 1.0, embedding_block, key_stack)
    return (embedding, pos_loss[None], neg_loss[None])


def solution(mesh):
    return jax.shard_map(
        per_device,
        mesh=mesh,
        in_specs=(
            P("row", None),
            P("row", "rep"),
            P("row", "rep"),
            P(),
            P(),
            P(),
            P("row", "rep", None),
            P("row", "rep", None),
        ),
        out_specs=(P(("row", "rep"), None), P("row", "rep", None), P("row", "rep", None)),
        check_vma=False,
    )
```

profile of v0, /device:TPU:36, one launch (start us, length us, event | category | flops | bytes accessed | tf_op | source)
XLA Modules:
  0.0 728.9 jit_solution(3178887019118339583)
XLA Ops:
  7.2 2.2 broadcast_select_fusion
  9.5 1.4 fusion.37
  13.5 265.5 %all-reduce.7.cloned.1.call-done = (bf16[768,256]{1,0:T(8,128)(2,1)}, bf16[768,256]{1,0:T(8,128)(2,1)}, bf16[768,256]{1,0:T(8,128)(2,1)}, bf16[768,256]{1,0:T(8,128)(2,1)}) async-done(((bf16[768,256]{1,0:T(8,128)(2,1)}, bf16[768,256]{1,0:T(8,128)(2,1)}, bf16[768,256]{1,0:T(8,128)(2,1)}, bf16[768,256]{1,0:T(8,128)(2,1)}), (bf16[768,256]{1,0:T(8,128)(2,1)}, bf16[768,256]{1,0:T(8,128)(2,1)}, ...) | async-done | bytes 1572880 | tf_op jit(solution)/shard_map/psum | solution.py:13
  279.0 2.0 convolution_select_fusion.3
  281.0 1.9 fusion.13
  282.9 1.9 fusion.12
  284.9 1.8 fusion.11
  286.7 1.2 copy.19
  287.9 0.9 fusion.20
  288.9 40.9 %reduce-scatter.4.cloned.1.call-done = f32[96,256]{1,0:T(8,128)} async-done(((f32[768,256]{1,0:T(8,128)}), f32[96,256]{1,0:T(8,128)}) %reduce-scatter.4.cloned.1.call-update) | async-done | bytes 98320
  329.8 1.0 copy.20
  330.8 0.3 multiply_reduce_fusion
  331.2 28.7 %all_gather.3 = bf16[768,256]{1,0:T(8,128)(2,1)S(1)} all-gather(bf16[96,256]{1,0:T(8,128)(2,1)S(1)} %multiply_convert_fusion), channel_id=1, replica_groups=mesh['row'=32,'rep'=8] {'rep'}, dimensions={0}, use_global_device_ids=true | all-gather | bytes 442368 | tf_op jit(solution)/shard_map/all_gather | solution.py:61
  359.9 1.2 select_bitcast_fusion.3
  361.3 6.5 gather_fusion
  367.8 6.6 gather_fusion.2
  374.4 253.7 %all-reduce.5.cloned.1.call-done = (bf16[1,768,256]{2,1,0:T(8,128)(2,1)}, bf16[1,768,256]{2,1,0:T(8,128)(2,1)}, bf16[1,768,256]{2,1,0:T(8,128)(2,1)}, bf16[1,768,256]{2,1,0:T(8,128)(2,1)}) async-done(((bf16[1,768,256]{2,1,0:T(8,128)(2,1)}, bf16[1,768,256]{2,1,0:T(8,128)(2,1)}, bf16[1,768,256]{2,1,0:T(8,128)(2,1)}, bf16[1,768,256]{2,1,0:T(8,128)(2,1)}), (bf16[1,768,256]{2,1,0:T(8,128)(2,1)}, ...) | async-done | bytes 1572880 | tf_op jit(solution)/shard_map/psum | solution.py:13
  628.1 1.5 pad_maximum_fusion
  629.7 1.2 copy.15
  630.9 30.4 %gather_fusion.1 = bf16[128,128,256]{2,0,1:T(8,128)(2,1)} fusion(bf16[4,768,256]{2,0,1:T(4,128)(2,1)S(1)} %copy.15, s32[128]{0:T(128)S(1)} %get-tuple-element.21), kind=kCustom, calls=%fused_computation.1 | custom fusion | bytes 16778752 | tf_op jit(solution)/shard_map/vmap()/gather | solution.py:33
  661.3 30.8 %gather_fusion.3 = bf16[128,128,256]{2,0,1:T(8,128)(2,1)} fusion(bf16[4,768,256]{2,0,1:T(4,128)(2,1)S(1)} %copy.15, s32[128]{0:T(128)S(1)} %get-tuple-element.19), kind=kCustom, calls=%fused_computation.3 | custom fusion | bytes 16778752 | tf_op jit(solution)/shard_map/vmap()/gather | solution.py:33
  692.1 14.7 %fusion = f32[128,128]{1,0:T(8,128)S(1)} fusion(bf16[128,128,256]{2,1,0:T(8,128)(2,1)} %gather_fusion, bf16[128,128,256]{2,0,1:T(8,128)(2,1)} %gather_fusion.1), kind=kOutput, calls=%fused_computation.6 | convolution fusion | flops 1090502656 | bytes 16842752 | tf_op jit(solution)/shard_map/pqf,pkf->pqk/dot_general | solution.py:38
  706.8 14.7 %fusion.1 = f32[128,128]{1,0:T(8,128)S(1)} fusion(bf16[128,128,256]{2,1,0:T(8,128)(2,1)} %gather_fusion.2, bf16[128,128,256]{2,0,1:T(8,128)(2,1)} %gather_fusion.3), kind=kOutput, calls=%fused_computation.7 | convolution fusion | flops 1090502656 | bytes 16842752 | tf_op jit(solution)/shard_map/pqf,pkf->pqk/dot_general | solution.py:38
  721.5 0.7 multiply_bitcast_fusion
  (28 shorter events, 0.3 us)
Async XLA Ops:
  7.2 323.6 %copy-start = (bf16[256,256]{1,0:T(8,128)(2,1)S(1)}, bf16[256,256]{1,0:T(8,128)(2,1)}, u32[]{:S(2)}) copy-start(bf16[256,256]{1,0:T(8,128)(2,1)} %param.12) | copy-start | bytes 393220
  7.2 271.8 %all-reduce.7.cloned.1.call-start = ((), (), s32[]{:S(2)}) async-start(), calls=%async_computation.3 | async-start | bytes 3145728 | tf_op jit(solution)/shard_map/psum | solution.py:13
  9.4 278.5 %copy-start.3 = (bf16[256,256]{1,0:T(8,128)(2,1)S(1)}, bf16[256,256]{1,0:T(8,128)(2,1)}, u32[]{:S(2)}) copy-start(bf16[256,256]{1,0:T(8,128)(2,1)} %param.11) | copy-start | bytes 393220
  9.4 321.4 %copy-start.6 = (f32[256]{0:T(256)S(1)}, f32[256]{0:T(256)}, u32[]{:S(2)}) copy-start(f32[256]{0:T(256)} %param.13) | copy-start | bytes 3076
  9.4 320.3 %reduce-scatter.4.cloned.1.call-start = ((), (), s32[]{:S(2)}) async-start(), calls=%async_computation.1 | async-start | bytes 884736
  279.0 5.8 copy-start.1
  281.0 80.2 %copy-start.4 = (s32[1,128,3]{1,0,2:T(1,128)S(1)}, s32[1,128,3]{1,0,2:T(1,128)}, u32[]{:S(2)}) copy-start(s32[1,128,3]{1,0,2:T(1,128)} %param.14) | copy-start | bytes 4612
  281.0 80.2 %copy-start.5 = (s32[1,128,3]{1,0,2:T(1,128)S(1)}, s32[1,128,3]{1,0,2:T(1,128)}, u32[]{:S(2)}) copy-start(s32[1,128,3]{1,0,2:T(1,128)} %param.15) | copy-start | bytes 4612
  287.8 340.3 %all-reduce.5.cloned.1.call-start = ((), (), s32[]{:S(2)}) async-start(), calls=%async_computation.2 | async-start | bytes 3145728 | tf_op jit(solution)/shard_map/psum | solution.py:13
  331.2 36.6 %copy-start.2 = (bf16[96,256]{1,0:T(8,128)(2,1)}, bf16[96,256]{1,0:T(8,128)(2,1)S(1)}, u32[]{:S(2)}) copy-start(bf16[96,256]{1,0:T(8,128)(2,1)S(1)} %multiply_convert_fusion) | copy-start | bytes 147460
Sparse Core Ops, SparseCore 0:
  10.9 268.0 all-reduce.6
  288.0 41.7 reduce-scatter.3
  361.3 266.8 all-reduce.4
where the time goes:
time: 741 us; the launch traced here: 729 us
  waiting for transfers between devices  560 us (76%)
  local copies, waits for them, and re-layouts  79.2 us (11%)
  matrix products  38.2 us (5%)
  blocking collectives  28.7 us (4%)
  between operations  16.7 us (2%)
    psum x2, waiting for transfers between devices, from_root(): return lax.psum(block, axis)  519 us
    gather x2, local copies, waits for them, and re-layouts, take_keys(): lax.dynamic_slice(key_stack, (section_id, offset, zero_index), (1, PAIR_R...  61.2 us
    unnamed x4, waiting for transfers between devices  41 us
    dot_general x2, matrix products, pair_losses(): jnp.einsum('pqf,pkf->pqk', queries, key_rows, preferred_element_type=jnp....  29.4 us
    all_gather x1, blocking collectives, per_device(): embedding_block = lax.all_gather(embedding, 'rep', axis=0, tiled=True)  28.7 us
  transfers between devices with their start and end apart: 3, of which 3 were waited for; matrix products, arithmetic and copies ran while one was open for 2% of the time, Pallas kernels for 0%

commit v1 on v0

v1 whole, which is shorter than its diff:
```python
import functools

import jax
import jax.numpy as jnp
from jax import lax
from jax.experimental import pallas as pl
from jax.experimental.pallas import tpu as pltpu
from jax.sharding import PartitionSpec as P

MESH = pl.DeviceIdType.MESH
N_Z, N_X, N_C, N_Y = 8, 4, 2, 2
N_REP = N_X * N_Y
TILE = 128
PART_TYPE = jnp.bfloat16


class Place:
    def __init__(self, yh, z, c, yl, x):
        self.yh, self.z, self.c, self.yl, self.x = yh, z, c, yl, x

    def moved(self, **kw):
        at = dict(self.__dict__)
        at.update(kw)
        return Place(**at)

    @property
    def device(self):
        return {
            "row": self.yh * (N_Z * N_C) + self.z * N_C + self.c,
            "rep": self.yl * N_X + self.x,
        }


def remote(src, dst, send_sem, recv_sem, place):
    return pltpu.make_async_remote_copy(
        src_ref=src, dst_ref=dst, send_sem=send_sem, recv_sem=recv_sem,
        device_id=place.device, device_id_type=MESH,
    )


class Spread:
    def __init__(self, me, piece, src, mid, full, sems):
        self.me, self.piece, self.src, self.mid, self.full = me, piece, src, mid, full
        self.s1, self.r1, self.s2, self.r2, self.s3, self.r3 = sems

    def rows(self, j, yl, c):
        block = (j % 2) * N_C + c
        at = block * (N_REP * self.piece) + (yl * N_X + j // 2) * self.piece
        return pl.ds(pl.multiple_of(at, 16), self.piece)

    def mid_rows(self, j):
        return pl.ds(pl.multiple_of(j * self.piece, 16), self.piece)

    def first(self, i):
        me = self.me
        d = (3 * i + 2 * me.x) % N_Z
        to = me.moved(z=(me.z + d) % N_Z, x=me.z // 2)
        stays = jnp.logical_and(d == 0, me.x == me.z // 2)
        j = me.x * 2 + me.z % 2
        copy = remote(self.src, self.mid.at[self.mid_rows(j), :], self.s1.at[i], self.r1.at[j], to)
        keep = pltpu.make_async_copy(self.src, self.mid.at[self.mid_rows(j), :], self.r1.at[j])
        return copy, keep, stays

    def start(self):
        for i in range(N_Z):
            copy, keep, stays = self.first(i)
            pl.when(stays)(keep.start)
            pl.when(jnp.logical_not(stays))(copy.start)

    def expected(self, t):
        me = self.me
        return (me.z + 2 * N_Z * 4 - 2 * me.x - 3 * t) % N_Z

    def second(self, j):
        me = self.me
        src = self.mid.at[self.mid_rows(j), :]
        dst = self.full.at[self.rows(j, me.yl, me.c), :]
        recv = self.r2.at[me.yl, j]
        far = remote(src, dst, self.s2.at[0, j], recv, me.moved(yh=1 - me.yh, yl=me.yh))
        near = remote(src, dst, self.s2.at[1, j], recv, me.moved(yl=me.yh))
        keep = pltpu.make_async_copy(src, dst, recv)
        return far, near, keep, me.yl == me.yh

    def relay(self, t):
        j = self.expected(t)
        arrived = self.mid.at[self.mid_rows(j), :]
        pltpu.make_async_copy(arrived, arrived, self.r1.at[j]).wait()
        far, near, keep, stays = self.second(j)
        far.start()
        pl.when(stays)(keep.start)
        pl.when(jnp.logical_not(stays))(near.start)

    def third(self, j, yl):
        me = self.me
        rows = self.full.at[self.rows(j, yl, me.c), :]
        return remote(rows, rows, self.s3.at[yl, j], self.r3.at[yl, j], me.moved(c=1 - me.c))

    def share(self, t):
        j = self.expected(t)
        for yl in range(N_Y):
            rows = self.full.at[self.rows(j, yl, self.me.c), :]
            pltpu.make_async_copy(rows, rows, self.r2.at[yl, j]).wait()
            self.third(j, yl).start()

    def wait_sibling(self, j):
        for yl in range(N_Y):
            rows = self.full.at[self.rows(j, yl, 1 - self.me.c), :]
            pltpu.make_async_copy(rows, rows, self.r3.at[yl, j]).wait()

    def finish(self):
        for i in range(N_Z):
            copy, _, stays = self.first(i)
            pl.when(jnp.logical_not(stays))(copy.wait_send)
        for j in range(N_Z):
            far, near, _, stays = self.second(j)
            far.wait_send()
            pl.when(jnp.logical_not(stays))(near.wait_send)
            for yl in range(N_Y):
                self.third(j, yl).wait_send()


LAG = 3


def kernel(
    live_ref, feat_ref, adj_ref, w_self_ref, w_neigh_ref, bias_ref, pos_ref, neg_ref,
    emb_ref, pos_loss_ref, neg_loss_ref,
    adj, mid_f, full_f, acc, part, got, own, mid_k, full_k, query, window, sums,
    adj_sem, f1s, f1r, f2s, f2r, f3s, f3r, k1s, k1r, k2s, k2r, k3s, k3r, ps, pr, qs, qr,
):
    row, rep = lax.axis_index("row"), lax.axis_index("rep")
    me = Place(row // (N_Z * N_C), (row // N_C) % N_Z, row % N_C, rep // N_X, rep % N_X)
    block, channels = feat_ref.shape
    piece = block // N_REP
    lists = pos_ref.shape[0]

    load = pltpu.make_async_copy(adj_ref, adj, adj_sem)
    load.start()

    barrier = pltpu.get_barrier_semaphore()

    def greet(place):
        pl.semaphore_signal(barrier, inc=1, device_id=place.device, device_id_type=MESH)

    for x in range(N_X):
        for zz in range(2):
            z = 2 * me.x + zz
            itself = jnp.logical_and(x == me.x, z == me.z)
            pl.when(jnp.logical_not(itself))(
                functools.partial(greet, me.moved(x=x, z=z))
            )
    for d in range(1, 4):
        y = (2 * me.yh + me.yl + d) % 4
        greet(me.moved(yh=y // 2, yl=y % 2))
    for d in range(1, N_REP):
        s = (rep + d) % N_REP
        greet(me.moved(yl=s // N_X, x=s % N_X))
    greet(me.moved(c=1 - me.c))
    targets = N_Z - (me.x == me.z // 2).astype(jnp.int32)
    pl.semaphore_wait(barrier, targets + 3 + (N_REP - 1) + 1)

    own_rows = pl.ds(pl.multiple_of(rep * piece, 16), piece)
    feats = Spread(me, piece, feat_ref.at[own_rows, :], mid_f, full_f, (f1s, f1r, f2s, f2r, f3s, f3r))
    feats.start()

    for section in range(4):
        column = lax.broadcasted_iota(jnp.int32, (lists, block), 1)
        for at, table in ((0, pos_ref), (lists, neg_ref)):
            first = jnp.where(table[:, 1:2] == section, table[:, 2:3], -block)
            inside = jnp.logical_and(column >= first, column < first + TILE)
            window[section, at : at + lists, :] = jnp.where(inside, 1.0, 0.0).astype(jnp.bfloat16)

    for t in range(N_Z + LAG):
        if t < N_Z:
            feats.relay(t)
        if t >= LAG:
            feats.share(t - LAG)

    load.wait()
    acc[...] = jnp.zeros_like(acc)

    def add_block(zz, c):
        k = zz * N_C + c
        at = pl.ds(pl.multiple_of(k * block, block), block)
        live = (live_ref[0, k] > 0).astype(jnp.float32).astype(jnp.bfloat16)
        acc[...] += jnp.dot(
            adj[:, at], full_f[at, :] * live, preferred_element_type=jnp.float32
        )

    for zz in range(2):
        add_block(zz, me.c)
    for zz in range(2):
        for x in range(N_X):
            feats.wait_sibling(x * 2 + zz)
        add_block(zz, 1 - me.c)

    part[...] = acc[...].astype(part.dtype)

    def partial_to(d):
        s = (rep + d) % N_REP
        return remote(
            part.at[pl.ds(pl.multiple_of(s * piece, 16), piece), :],
            got.at[d - 1], ps.at[d - 1], pr.at[d - 1], me.moved(yl=s // N_X, x=s % N_X),
        )

    for d in range(1, N_REP):
        partial_to(d).start()
    projected = jnp.dot(feat_ref[own_rows, :], w_self_ref[...], preferred_element_type=jnp.float32)
    neighbour = acc[own_rows, :]
    for d in range(1, N_REP):
        partial_to(d).wait_recv()
        neighbour = neighbour + got[d - 1].astype(jnp.float32)
    projected = projected + jnp.dot(
        neighbour.astype(jnp.bfloat16), w_neigh_ref[...], preferred_element_type=jnp.float32
    )
    projected = projected + bias_ref[...]
    scaled = projected * lax.rsqrt(jnp.mean(projected * projected, axis=-1, keepdims=True) + 1e-06)
    own[...] = scaled.astype(jnp.bfloat16)
    emb_ref[...] = own[...]

    def query_to(d):
        s = (rep + d) % N_REP
        return remote(
            own, query.at[own_rows, :], qs.at[d - 1], qr.at[d - 1], me.moved(yl=s // N_X, x=s % N_X)
        )

    keys = Spread(me, piece, own, mid_k, full_k, (k1s, k1r, k2s, k2r, k3s, k3r))
    keys.start()
    for d in range(1, N_REP):
        query_to(d).start()
    query[own_rows, :] = own[...]

    for t in range(N_Z + LAG):
        if t < N_Z:
            keys.relay(t)
        if t >= LAG:
            keys.share(t - LAG)
    for d in range(1, N_REP):
        query_to(d).wait_recv()

    sums[...] = jnp.zeros_like(sums)
    step = 2 * TILE

    def score_block(zz, c):
        k = zz * N_C + c
        for m in range(0, block, step):
            at = pl.ds(pl.multiple_of(k * block + m, step), step)
            scores = lax.dot_general(
                full_k[at, :], query[...], (((1,), (1,)), ((), ())),
                preferred_element_type=jnp.float32,
            ) * (channels ** -0.5)
            tail = jnp.log1p(jnp.exp(-jnp.abs(scores)))
            down = (tail + jnp.maximum(-scores, 0.0)).astype(jnp.bfloat16)
            up = (tail + jnp.maximum(scores, 0.0)).astype(jnp.bfloat16)
            sums[:lists, :] += jnp.dot(
                window[k, :lists, m : m + step], down, preferred_element_type=jnp.float32
            )
            sums[lists:, :] += jnp.dot(
                window[k, lists:, m : m + step], up, preferred_element_type=jnp.float32
            )

    for zz in range(2):
        score_block(zz, me.c)
    for zz in range(2):
        for x in range(N_X):
            keys.wait_sibling(x * 2 + zz)
        score_block(zz, 1 - me.c)

    for at, table, out_ref in ((0, pos_ref, pos_loss_ref), (lists, neg_ref, neg_loss_ref)):
        loss = jnp.zeros((lists, TILE), jnp.float32)
        for q in range(block // TILE):
            tile = sums[at : at + lists, q * TILE : (q + 1) * TILE]
            loss = jnp.where(table[:, 0:1] == q, tile, loss)
        out_ref[...] = loss * (1.0 / TILE)

    feats.finish()
    keys.finish()
    for d in range(1, N_REP):
        partial_to(d).wait_send()
        query_to(d).wait_send()


def per_device(features, adjacency, tile_live, w_self, w_neigh, bias_vector, pos_pairs, neg_pairs):
    block, channels = features.shape
    sources = adjacency.shape[1]
    piece = block // N_REP
    lists = pos_pairs.shape[1]
    vmem = pl.BlockSpec(memory_space=pltpu.VMEM)
    dma = pltpu.SemaphoreType.DMA
    spread_sems = [dma((N_Z,)), dma((N_Z,)), dma((2, N_Z)), dma((2, N_Z)), dma((2, N_Z)), dma((2, N_Z))]
    bf16 = jnp.bfloat16
    embedding, pos_loss, neg_loss = pl.pallas_call(
        kernel,
        out_shape=(
            jax.ShapeDtypeStruct((piece, channels), bf16),
            jax.ShapeDtypeStruct((lists, TILE), jnp.float32),
            jax.ShapeDtypeStruct((lists, TILE), jnp.float32),
        ),
        in_specs=[
            pl.BlockSpec(memory_space=pltpu.SMEM), vmem, pl.BlockSpec(memory_space=pl.ANY),
            vmem, vmem, vmem, vmem, vmem,
        ],
        out_specs=(vmem, vmem, vmem),
        scratch_shapes=[
            pltpu.VMEM((block, sources), bf16),
            pltpu.VMEM((N_Z * piece, channels), bf16),
            pltpu.VMEM((sources, channels), bf16),
            pltpu.VMEM((block, channels), jnp.float32),
            pltpu.VMEM((block, channels), PART_TYPE),
            pltpu.VMEM((N_REP - 1, piece, channels), PART_TYPE),
            pltpu.VMEM((piece, channels), bf16),
            pltpu.VMEM((N_Z * piece, channels), bf16),
            pltpu.VMEM((sources, channels), bf16),
            pltpu.VMEM((block, channels), bf16),
            pltpu.VMEM((4, 2 * lists, block), bf16),
            pltpu.VMEM((2 * lists, block), jnp.float32),
            dma(()),
            *spread_sems,
            *spread_sems,
            dma((N_REP - 1,)), dma((N_REP - 1,)), dma((N_REP - 1,)), dma((N_REP - 1,)),
        ],
        compiler_params=pltpu.CompilerParams(
            collective_id=0, has_side_effects=True, vmem_limit_bytes=40 * 1024 * 1024
        ),
    )(
        tile_live, features, adjacency, w_self, w_neigh, bias_vector.reshape(1, channels),
        pos_pairs[0], neg_pairs[0],
    )
    return embedding, pos_loss[None], neg_loss[None]


def solution(mesh):
    return jax.shard_map(
        per_device,
        mesh=mesh,
        in_specs=(
            P("row", None),
            P("row", "rep"),
            P("row", "rep"),
            P(),
            P(),
            P(),
            P("row", "rep", None),
            P("row", "rep", None),
        ),
        out_specs=(P(("row", "rep"), None), P("row", "rep", None), P("row", "rep", None)),
        check_vma=False,
    )
```

time: 741 us -> 89.2 us (0.12); the launches traced: 729 us -> 89 us
  waiting for transfers between devices: 560 us -> 0 us
  Pallas kernels: 0 us -> 78.4 us
  local copies, waits for them, and re-layouts: 79.2 us -> 9.92 us
  matrix products: 38.2 us -> 0 us
  blocking collectives: 28.7 us -> 0 us
  between operations: 16.7 us -> 0.65 us
    psum x2 -> x0, waiting for transfers between devices: 519 us -> none  [from_root(): return lax.psum(block, axis)]
    pallas_call x0 -> x1, Pallas kernels: none -> 78.4 us  [per_device(): pl.pallas_call(kernel, out_shape=(jax.ShapeDtypeStruct((piece, channels),...]
    gather x4 -> x0, local copies, waits for them, and re-layouts: 74.4 us -> none  [the longest x2 61.2 us: take_keys(): lax.dynamic_slice(key_stack, (section_id, offset, zero_index), (1, PAIR_R...]
    unnamed x4 -> x0, waiting for transfers between devices: 41 us -> none
    dot_general x8 -> x0, matrix products: 38.2 us -> none  [the longest x2 29.4 us: pair_losses(): jnp.einsum('pqf,pkf->pqk', queries, key_rows, preferred_element_type=jnp....]
    all_gather x1 -> x0, blocking collectives: 28.7 us -> none  [per_device(): embedding_block = lax.all_gather(embedding, 'rep', axis=0, tiled=True)]
    unnamed x18 -> x17, local copies, waits for them, and re-layouts: 2.2 us -> 9.92 us
  transfers between devices with their start and end apart: 3 -> 0, of which waited for: 3 -> 0; matrix products, arithmetic and copies ran while one was open for 2% -> 0% of each run, Pallas kernels for 0% -> 0%
where the time goes in v1:
time: 89.2 us; the launch traced here: 89 us
  Pallas kernels  78.4 us (88%)
  local copies, waits for them, and re-layouts  9.92 us (11%)
    pallas_call x1, Pallas kernels, per_device(): pl.pallas_call(kernel, out_shape=(jax.ShapeDtypeStruct((piece, channels),...  78.4 us
    unnamed x17, local copies, waits for them, and re-layouts  9.92 us

profile of v1, /device:TPU:36, one launch (start us, length us, event | category | flops | bytes accessed | tf_op | source)
XLA Modules:
  0.0 89.0 jit_solution(14873676640469977772)
XLA Ops:
  0.6 0.8 copy.11
  1.4 0.8 copy.12
  2.2 0.0 copy-start
  2.2 2.3 %copy-done = bf16[768,3072]{1,0:T(8,128)(2,1)S(1)} copy-done((bf16[768,3072]{1,0:T(8,128)(2,1)S(1)}, bf16[768,3072]{1,0:T(8,128)(2,1)}, u32[]{:S(2)}) %copy-start) | copy-done | bytes 4718616
  4.5 0.0 copy-start.1
  4.5 1.0 %copy-done.1 = bf16[768,256]{1,0:T(8,128)(2,1)S(1)} copy-done((bf16[768,256]{1,0:T(8,128)(2,1)S(1)}, bf16[768,256]{1,0:T(8,128)(2,1)}, u32[]{:S(2)}) %copy-start.1) | copy-done | bytes 393240
  5.5 0.0 copy-start.2
  5.5 0.9 %copy-done.2 = bf16[256,256]{1,0:T(8,128)(2,1)S(1)} copy-done((bf16[256,256]{1,0:T(8,128)(2,1)S(1)}, bf16[256,256]{1,0:T(8,128)(2,1)}, u32[]{:S(2)}) %copy-start.2) | copy-done | bytes 131096
  6.4 0.0 copy-start.3
  6.4 0.9 %copy-done.3 = bf16[256,256]{1,0:T(8,128)(2,1)S(1)} copy-done((bf16[256,256]{1,0:T(8,128)(2,1)S(1)}, bf16[256,256]{1,0:T(8,128)(2,1)}, u32[]{:S(2)}) %copy-start.3) | copy-done | bytes 131096
  7.3 0.0 copy-start.4
  7.3 0.7 copy-done.4
  8.0 0.0 copy-start.5
  8.0 0.7 copy-done.5
  8.7 78.4 %shard_map.103 = (bf16[96,256]{1,0:T(8,128)(2,1)S(1)}, f32[128,128]{1,0:T(8,128)S(1)}, f32[128,128]{1,0:T(8,128)S(1)}) custom-call(s32[1,4]{1,0:T(1,128)S(1)} %copy-done.5, bf16[768,256]{1,0:T(8,128)(2,1)S(1)} %copy-done.1, bf16[768,3072]{1,0:T(8,128)(2,1)S(1)} %copy-done, bf16[256,256]{1,0:T(8,128)(2,1)S(1)} %copy-done.2, bf16[256,256]{1,0:T(8,128)(2,1)S(1)} %copy-done.3, ...), custom_call_target="tpu_custom_call" | custom-call | tf_op jit(solution)/shard_map/pallas_call | solution.py:292
  87.1 0.6 copy.16
  87.7 0.6 copy.17
  88.3 0.6 copy.18
Async XLA Ops:
  2.2 2.3 %copy-start = (bf16[768,3072]{1,0:T(8,128)(2,1)S(1)}, bf16[768,3072]{1,0:T(8,128)(2,1)}, u32[]{:S(2)}) copy-start(bf16[768,3072]{1,0:T(8,128)(2,1)} %adj_ref.1) | copy-start | bytes 14155780
  4.5 1.0 %copy-start.1 = (bf16[768,256]{1,0:T(8,128)(2,1)S(1)}, bf16[768,256]{1,0:T(8,128)(2,1)}, u32[]{:S(2)}) copy-start(bf16[768,256]{1,0:T(8,128)(2,1)} %feat_ref.1) | copy-start | bytes 1179652
  5.5 0.9 %copy-start.2 = (bf16[256,256]{1,0:T(8,128)(2,1)S(1)}, bf16[256,256]{1,0:T(8,128)(2,1)}, u32[]{:S(2)}) copy-start(bf16[256,256]{1,0:T(8,128)(2,1)} %w_self_ref.1) | copy-start | bytes 393220
  6.4 0.9 %copy-start.3 = (bf16[256,256]{1,0:T(8,128)(2,1)S(1)}, bf16[256,256]{1,0:T(8,128)(2,1)}, u32[]{:S(2)}) copy-start(bf16[256,256]{1,0:T(8,128)(2,1)} %w_neigh_ref.1) | copy-start | bytes 393220
  7.3 0.7 copy-start.4
  8.0 0.7 copy-start.5

commit v2 on v0

v2 whole, which is shorter than its diff:
```python
import functools

import jax
import jax.numpy as jnp
from jax import lax
from jax.experimental import pallas as pl
from jax.experimental.pallas import tpu as pltpu
from jax.sharding import PartitionSpec as P

MESH = pl.DeviceIdType.MESH
N_Z, N_X, N_C, N_Y = 8, 4, 2, 2
N_REP = N_X * N_Y
TILE = 128
PART_TYPE = jnp.bfloat16


class Place:
    def __init__(self, yh, z, c, yl, x):
        self.yh, self.z, self.c, self.yl, self.x = yh, z, c, yl, x

    def moved(self, **kw):
        at = dict(self.__dict__)
        at.update(kw)
        return Place(**at)

    @property
    def device(self):
        return {
            "row": self.yh * (N_Z * N_C) + self.z * N_C + self.c,
            "rep": self.yl * N_X + self.x,
        }


def remote(src, dst, send_sem, recv_sem, place):
    return pltpu.make_async_remote_copy(
        src_ref=src, dst_ref=dst, send_sem=send_sem, recv_sem=recv_sem,
        device_id=place.device, device_id_type=MESH,
    )


def arrived(ref, sem):
    pltpu.make_async_copy(ref, ref, sem).wait()


class Spread:
    HOPS = [(dz, other) for other in (1, 0) for dz in (2, 1, -1, 0)]

    def __init__(self, me, piece, src, mirror, full, sems):
        self.me, self.piece, self.src, self.mirror, self.full = me, piece, src, mirror, full
        self.s1, self.r1, self.s2, self.r2, self.s3, self.r3 = sems

    def unit(self, zz, c, yl):
        rows = N_X * self.piece
        at = ((zz * N_C + c) * N_Y + yl) * rows
        return self.full.at[pl.ds(pl.multiple_of(at, TILE), rows), :]

    def slot(self, zz, yl, x):
        at = (((zz * N_C + self.me.c) * N_Y + yl) * N_X + x) * self.piece
        return self.full.at[pl.ds(pl.multiple_of(at, 16), self.piece), :]

    def plane(self, source, dz):
        return (source + N_Z + dz * (1 - 2 * self.me.c)) % N_Z

    def to_mirror(self):
        me = self.me
        return remote(self.src, self.mirror, self.s1, self.r1, me.moved(z=(me.z + 4) % N_Z))

    def copies(self, relayed):
        me = self.me
        source = (me.z + 4 * relayed) % N_Z
        src = self.mirror if relayed else self.src
        dst = self.slot(source % 2, me.yl, me.x)
        recv = self.r2.at[(source % 2), me.yl, me.x]
        for i, (dz, other) in enumerate(self.HOPS):
            to = me.moved(
                x=source // 2, yl=me.yh, yh=1 - me.yh if other else me.yh, z=self.plane(me.z, dz)
            )
            copy = remote(src, dst, self.s2.at[relayed, i], recv, to)
            if dz == 0 and not other:
                stays = jnp.logical_and(me.x == source // 2, me.yl == me.yh)
                yield copy, pltpu.make_async_copy(src, dst, recv), stays
            else:
                yield copy, None, None

    def send(self, relayed):
        for copy, keep, stays in self.copies(relayed):
            if keep is None:
                copy.start()
            else:
                pl.when(stays)(keep.start)
                pl.when(jnp.logical_not(stays))(copy.start)

    def start(self):
        self.to_mirror().start()
        self.send(0)

    def relay(self):
        self.to_mirror().wait_recv()
        self.send(1)

    def away(self, source, c):
        dz = (self.me.z + N_Z - source) % N_Z
        return jnp.where(c == 0, dz, (N_Z - dz) % N_Z)

    @staticmethod
    def direct(away):
        return jnp.logical_or(away <= 2, away == N_Z - 1)

    def order(self, i, c):
        first = jnp.where(self.direct(self.away(2 * self.me.x, c)), 0, 1)
        return jnp.where(i < 2, first, 1 - first), i % 2

    def to_sibling(self, zz, yl):
        me = self.me
        rows = self.unit(zz, me.c, yl)
        return remote(rows, rows, self.s3.at[zz, yl], self.r3.at[zz, yl], me.moved(c=1 - me.c))

    def take_own(self, zz, yl):
        for x in range(N_X):
            arrived(self.slot(zz, yl, x), self.r2.at[zz, yl, x])
        self.to_sibling(zz, yl).start()

    def take_sibling(self, zz, yl):
        arrived(self.unit(zz, 1 - self.me.c, yl), self.r3.at[zz, yl])

    def finish(self):
        self.to_mirror().wait_send()
        for relayed in range(2):
            for copy, keep, stays in self.copies(relayed):
                if keep is None:
                    copy.wait_send()
                else:
                    pl.when(jnp.logical_not(stays))(copy.wait_send)
        for zz in range(2):
            for yl in range(N_Y):
                self.to_sibling(zz, yl).wait_send()

    def greet(self, greet):
        me = self.me
        greet(me.moved(z=(me.z + 4) % N_Z))
        for zz in range(2):
            source = 2 * me.x + zz
            dz = self.away(source, me.c)
            z = jnp.where(self.direct(dz), source, (source + 4) % N_Z)
            for yl in range(N_Y):
                for x in range(N_X):
                    itself = jnp.logical_and(
                        jnp.logical_and(x == me.x, yl == me.yl),
                        jnp.logical_and(z == me.z, me.yh == me.yl),
                    )
                    pl.when(jnp.logical_not(itself))(
                        functools.partial(greet, me.moved(x=x, z=z, yl=yl, yh=me.yl))
                    )
        targets = 1
        for relayed in range(2):
            source = (me.z + 4 * relayed) % N_Z
            stays = jnp.logical_and(me.x == source // 2, me.yl == me.yh)
            targets = targets + len(self.HOPS) - stays.astype(jnp.int32)
        return targets


def each_unit(spread, work):
    def take(p, n):
        own = jnp.logical_or(p < 2, jnp.logical_or(p == 3, p == 5))
        i = jnp.where(own, (p + 1) // 2, (p - 1) // 2)
        i = jnp.where(p == 7, 3, i)
        c = jnp.where(own, spread.me.c, 1 - spread.me.c)
        zz, yl = spread.order(i, c)
        pl.when(own)(lambda: spread.take_own(zz, yl))
        pl.when(jnp.logical_not(own))(lambda: spread.take_sibling(zz, yl))
        work(zz, c, yl, n)

    def step(p, carry):
        take(2 * p, 0)
        take(2 * p + 1, 1)
        return carry

    lax.fori_loop(0, 4, step, 0)


def kernel(
    live_ref, feat_ref, adj_ref, w_self_ref, w_neigh_ref, bias_ref, pos_ref, neg_ref,
    emb_ref, loss_ref,
    adj, feat, w_self, w_neigh, bias, tables, live, picks,
    mirror_f, full_f, acc, part, got, own, mirror_k, full_k, query, query_t, window, down_0, up_0, down_1, up_1, last, sums,
    losses, load_sem, store_sem, f1s, f1r, f2s, f2r, f3s, f3r, k1s, k1r, k2s, k2r, k3s, k3r, ps, pr, qs, qr,
):
    row, rep = lax.axis_index("row"), lax.axis_index("rep")
    me = Place(row // (N_Z * N_C), (row // N_C) % N_Z, row % N_C, rep // N_X, rep % N_X)
    block, channels = feat_ref.shape
    piece = block // N_REP
    lists = pos_ref.shape[2]
    own_rows = pl.ds(pl.multiple_of(rep * piece, 16), piece)
    loads = [
        pltpu.make_async_copy(src, dst, load_sem.at[i])
        for i, (src, dst) in enumerate((
            (feat_ref.at[own_rows, :], feat), (pos_ref, tables.at[0]), (neg_ref, tables.at[1]),
            (live_ref, live), (adj_ref, adj),
            (w_self_ref, w_self), (w_neigh_ref, w_neigh), (bias_ref, bias),
        ))
    ]
    for load in loads:
        load.start()
    feats = Spread(me, piece, feat, mirror_f, full_f, (f1s, f1r, f2s, f2r, f3s, f3r))
    keys = Spread(me, piece, own, mirror_k, full_k, (k1s, k1r, k2s, k2r, k3s, k3r))
    pending = []

    barrier = pltpu.get_barrier_semaphore()

    def greet(place):
        pl.semaphore_signal(barrier, inc=1, device_id=place.device, device_id_type=MESH)

    targets = feats.greet(greet)
    for d in range(1, N_REP):
        s = (rep + d) % N_REP
        greet(me.moved(yl=s // N_X, x=s % N_X))
    greet(me.moved(c=1 - me.c))
    loads[0].wait()
    pl.semaphore_wait(barrier, targets + (N_REP - 1) + 1)

    feats.start()

    def down_rows(row):
        wide = jnp.broadcast_to(row, (row.shape[1], row.shape[1]))
        return jnp.transpose(wide.astype(jnp.float32)).astype(jnp.int32)

    for load in loads[1:3]:
        load.wait()
    column = lax.broadcasted_iota(jnp.int32, (lists, TILE), 1)
    for half in range(2):
        at = half * lists
        picks[at : at + lists, :] = down_rows(tables[half, 0])
        first = down_rows(tables[half, 1] * block + tables[half, 2])

        def fill(i, carry):
            for j in range(0, window.shape[2], TILE):
                since = column + (i * window.shape[2] + j) - first
                inside = jnp.logical_and(since >= 0, since < TILE)
                window[i, at : at + lists, j : j + TILE] = jnp.where(inside, 1.0, 0.0).astype(
                    jnp.bfloat16
                )
            return carry

        lax.fori_loop(0, window.shape[0], fill, 0)
    acc[...] = jnp.zeros_like(acc)
    sums[...] = jnp.zeros_like(sums)

    feats.relay()
    for load in loads[3:]:
        load.wait()

    half_block = N_X * piece

    def aggregate(zz, c, yl, n):
        k = zz * N_C + c
        flag = (live[0, k] > 0).astype(jnp.float32).astype(jnp.bfloat16)
        at = pl.ds(pl.multiple_of(k * block + yl * half_block, TILE), half_block)
        acc[...] += jnp.dot(
            adj[:, at], full_f[at, :] * flag, preferred_element_type=jnp.float32
        )

    each_unit(feats, aggregate)
    pending.append(feats.finish)

    part[...] = acc[...].astype(part.dtype)

    def partial_to(d):
        s = (rep + d) % N_REP
        return remote(
            part.at[pl.ds(pl.multiple_of(s * piece, 16), piece), :],
            got.at[d - 1], ps.at[d - 1], pr.at[d - 1], me.moved(yl=s // N_X, x=s % N_X),
        )

    for d in range(1, N_REP):
        partial_to(d).start()
    pending.extend(partial_to(d).wait_send for d in range(1, N_REP))
    projected = jnp.dot(feat[...], w_self[...], preferred_element_type=jnp.float32)
    neighbour = acc[own_rows, :]
    for d in range(1, N_REP):
        partial_to(d).wait_recv()
        neighbour = neighbour + got[d - 1].astype(jnp.float32)
    projected = projected + jnp.dot(
        neighbour.astype(jnp.bfloat16), w_neigh[...], preferred_element_type=jnp.float32
    )
    projected = projected + bias[...]
    scaled = projected * lax.rsqrt(jnp.mean(projected * projected, axis=-1, keepdims=True) + 1e-06)
    own[...] = scaled.astype(jnp.bfloat16)

    def query_to(d):
        s = (rep + d) % N_REP
        return remote(
            own, query.at[own_rows, :], qs.at[d - 1], qr.at[d - 1], me.moved(yl=s // N_X, x=s % N_X)
        )

    keys.start()
    for d in range(1, N_REP):
        query_to(d).start()
    pending.extend(query_to(d).wait_send for d in range(1, N_REP))
    query[own_rows, :] = own[...]
    store_emb = pltpu.make_async_copy(own, emb_ref, store_sem.at[0])
    store_emb.start()
    pending.append(store_emb.wait)

    keys.relay()
    for d in range(1, N_REP):
        query_to(d).wait_recv()
    scale = channels ** -0.5
    query_t[...] = (jnp.transpose(query[...].astype(jnp.float32)) * scale).astype(jnp.bfloat16)


    soft = ((down_0, up_0), (down_1, up_1))

    def add_windows(down, up):
        unit = last[0]
        rows = window[unit]
        sums[:lists, :] += jnp.dot(rows[:lists], down[...], preferred_element_type=jnp.float32)
        sums[lists:, :] += jnp.dot(rows[lists:], up[...], preferred_element_type=jnp.float32)

    def score(zz, c, yl, n):
        unit = (zz * N_C + c) * N_Y + yl
        add_windows(*soft[1 - n])
        down, up = soft[n]
        for j in range(half_block // TILE):
            at = pl.ds(pl.multiple_of(unit * half_block + j * TILE, TILE), TILE)
            rows = slice(j * TILE, (j + 1) * TILE)
            t = jnp.dot(full_k[at, :], query_t[...], preferred_element_type=jnp.float32)
            low, high = jnp.minimum(t, 0.0), jnp.maximum(t, 0.0)
            e = jnp.exp(low - high)
            tail = jnp.where(e < 2.0 ** -12, e, jnp.log(1.0 + e))
            down[rows, :] = (tail - low).astype(jnp.bfloat16)
            up[rows, :] = (tail + high).astype(jnp.bfloat16)
        last[0] = unit

    for ref in soft[1]:
        ref[...] = jnp.zeros_like(ref)
    last[0] = 0
    each_unit(keys, score)
    add_windows(*soft[1])
    pending.append(keys.finish)

    for half in range(2):
        at = half * lists
        loss = jnp.zeros((lists, TILE), jnp.float32)
        for q in range(block // TILE):
            tile = sums[at : at + lists, q * TILE : (q + 1) * TILE]
            loss = jnp.where(picks[at : at + lists, :] == q, tile, loss)
        losses[half] = loss * (1.0 / TILE)
    store_loss = pltpu.make_async_copy(losses, loss_ref, store_sem.at[1])
    store_loss.start()
    pending.append(store_loss.wait)
    for wait in pending:
        wait()


def hand_out(emb_in, loss_in, emb_ref, pos_ref, neg_ref):
    emb_ref[...] = emb_in[...]
    pos_ref[...] = loss_in[0]
    neg_ref[...] = loss_in[1]


def per_device(features, adjacency, tile_live, w_self, w_neigh, bias_vector, pos_pairs, neg_pairs):
    block, channels = features.shape
    sources = adjacency.shape[1]
    piece = block // N_REP
    lists = pos_pairs.shape[1]
    table = (pos_pairs.shape[2], 1, lists)
    place = pl.BlockSpec(memory_space=pl.ANY)
    vmem = pl.BlockSpec(memory_space=pltpu.VMEM)
    dma = pltpu.SemaphoreType.DMA
    spread_sems = [
        dma(()), dma(()), dma((2, 8)), dma((2, N_Y, N_X)), dma((2, N_Y)), dma((2, N_Y)),
    ]
    bf16 = jnp.bfloat16
    f32 = jnp.float32
    limit = 60 * 1024 * 1024
    embedding, losses = pl.pallas_call(
        kernel,
        out_shape=(
            jax.ShapeDtypeStruct((piece, channels), bf16),
            jax.ShapeDtypeStruct((2, lists, TILE), f32),
        ),
        in_specs=[place] * 8,
        out_specs=(place,) * 2,
        scratch_shapes=[
            pltpu.VMEM((block, sources), bf16),
            pltpu.VMEM((piece, channels), bf16),
            pltpu.VMEM((channels, channels), bf16),
            pltpu.VMEM((channels, channels), bf16),
            pltpu.VMEM((1, channels), jnp.float32),
            pltpu.VMEM((2, *table), jnp.int32),
            pltpu.SMEM((1, 4), jnp.int32),
            pltpu.VMEM((2 * lists, lists), jnp.int32),
            pltpu.VMEM((piece, channels), bf16),
            pltpu.VMEM((sources, channels), bf16),
            pltpu.VMEM((block, channels), jnp.float32),
            pltpu.VMEM((block, channels), PART_TYPE),
            pltpu.VMEM((N_REP - 1, piece, channels), PART_TYPE),
            pltpu.VMEM((piece, channels), bf16),
            pltpu.VMEM((piece, channels), bf16),
            pltpu.VMEM((sources, channels), bf16),
            pltpu.VMEM((block, channels), bf16),
            pltpu.VMEM((channels, block), bf16),
            pltpu.VMEM((8, 2 * lists, block // 2), bf16),
            *[pltpu.VMEM((block // 2, block), bf16)] * 4,
            pltpu.SMEM((1,), jnp.int32),
            pltpu.VMEM((2 * lists, block), jnp.float32),
            pltpu.VMEM((2, lists, TILE), f32),
            dma((8,)), dma((2,)),
            *spread_sems,
            *spread_sems,
            dma((N_REP - 1,)), dma((N_REP - 1,)), dma((N_REP - 1,)), dma((N_REP - 1,)),
        ],
        compiler_params=pltpu.CompilerParams(
            collective_id=0, has_side_effects=True, vmem_limit_bytes=limit
        ),
    )(
        tile_live, features, adjacency, w_self, w_neigh, bias_vector.reshape(1, channels),
        pos_pairs.transpose(2, 0, 1), neg_pairs.transpose(2, 0, 1),
    )
    embedding, pos_loss, neg_loss = pl.pallas_call(
        hand_out,
        out_shape=(
            jax.ShapeDtypeStruct((piece, channels), bf16),
            jax.ShapeDtypeStruct((lists, TILE), f32),
            jax.ShapeDtypeStruct((lists, TILE), f32),
        ),
        in_specs=[vmem] * 2,
        out_specs=(vmem,) * 3,
        compiler_params=pltpu.CompilerParams(vmem_limit_bytes=limit),
    )(embedding, losses)
    return embedding, pos_loss[None], neg_loss[None]


def solution(mesh):
    return jax.shard_map(
        per_device,
        mesh=mesh,
        in_specs=(
            P("row", None),
            P("row", "rep"),
            P("row", "rep"),
            P(),
            P(),
            P(),
            P("row", "rep", None),
            P("row", "rep", None),
        ),
        out_specs=(P(("row", "rep"), None), P("row", "rep", None), P("row", "rep", None)),
        check_vma=False,
    )
```

time: 741 us -> 77.4 us (0.10)
  the two profiles are of different devices: /device:TPU:36 before, /device:TPU:32 now
where the time goes in v2:
time: 77.4 us; the launch traced here: 77.3 us
  Pallas kernels  76.7 us (99%)
    pallas_call x1, Pallas kernels, per_device(): pl.pallas_call(kernel, out_shape=(jax.ShapeDtypeStruct((piece, channels),...  75.1 us
    pallas_call x1, Pallas kernels, per_device(): pl.pallas_call(hand_out, out_shape=(jax.ShapeDtypeStruct((piece, channels...  1.61 us

profile of v2, /device:TPU:32, one launch (start us, length us, event | category | flops | bytes accessed | tf_op | source)
XLA Modules:
  0.0 77.3 jit_solution(13423606954933275706)
XLA Ops:
  0.6 75.1 %shard_map.103 = (bf16[96,256]{1,0:T(8,128)(2,1)}, f32[2,128,128]{2,1,0:T(8,128)}) custom-call(s32[1,4]{1,0:T(1,128)} %live_ref.1, bf16[768,256]{1,0:T(8,128)(2,1)} %feat_ref.1, bf16[768,3072]{1,0:T(8,128)(2,1)} %adj_ref.1, bf16[256,256]{1,0:T(8,128)(2,1)} %w_self_ref.1, bf16[256,256]{1,0:T(8,128)(2,1)} %w_neigh_ref.1, f32[1,256]{1,0:T(1,128)} %bitcast.7, ...), custom_call_target="tpu_custom_call" | custom-call | tf_op jit(solution)/shard_map/pallas_call | solution.py:376
  75.7 1.6 %shard_map.104 = (bf16[96,256]{1,0:T(8,128)(2,1)}, f32[128,128]{1,0:T(8,128)}, f32[128,128]{1,0:T(8,128)}) custom-call(bf16[96,256]{1,0:T(8,128)(2,1)} %get-tuple-element.8.emb_in, f32[2,128,128]{2,1,0:T(8,128)} %get-tuple-element.9.loss_in), custom_call_target="tpu_custom_call" | custom-call | tf_op jit(solution)/shard_map/pallas_call | solution.py:420

commit v3 on v2

v3 whole, which is shorter than its diff:
```python
import functools

import jax
import jax.numpy as jnp
from jax import lax
from jax.experimental import pallas as pl
from jax.experimental.pallas import tpu as pltpu
from jax.sharding import PartitionSpec as P

MESH = pl.DeviceIdType.MESH
N_Z, N_X, N_C, N_Y = 8, 4, 2, 2
N_REP = N_X * N_Y
TILE = 128
PART_TYPE = jnp.bfloat16


class Place:
    def __init__(self, yh, z, c, yl, x):
        self.yh, self.z, self.c, self.yl, self.x = yh, z, c, yl, x

    def moved(self, **kw):
        at = dict(self.__dict__)
        at.update(kw)
        return Place(**at)

    @property
    def device(self):
        return {
            "row": self.yh * (N_Z * N_C) + self.z * N_C + self.c,
            "rep": self.yl * N_X + self.x,
        }


def remote(src, dst, send_sem, recv_sem, place):
    return pltpu.make_async_remote_copy(
        src_ref=src, dst_ref=dst, send_sem=send_sem, recv_sem=recv_sem,
        device_id=place.device, device_id_type=MESH,
    )


def arrived(ref, sem):
    pltpu.make_async_copy(ref, ref, sem).wait()


class Spread:
    STEPS = (2, 1, -1, 0)

    def __init__(self, me, piece, held, full, sems):
        self.me, self.piece, self.held, self.full = me, piece, held, full
        self.s1, self.r1, self.s2, self.r2, self.s3, self.r3 = sems
        self.outer = me.yl == me.yh
        self.twin = me.moved(yh=1 - me.yh, yl=1 - me.yl)

    def unit(self, zz, c, yl):
        rows = N_X * self.piece
        at = ((zz * N_C + c) * N_Y + yl) * rows
        return self.full.at[pl.ds(pl.multiple_of(at, TILE), rows), :]

    def slot(self, zz, yl, x):
        at = (((zz * N_C + self.me.c) * N_Y + yl) * N_X + x) * self.piece
        return self.full.at[pl.ds(pl.multiple_of(at, 16), self.piece), :]

    def plane(self, source, dz):
        return (source + N_Z + dz * (1 - 2 * self.me.c)) % N_Z

    def mirrored(self):
        me, twin = self.me, self.twin
        return me.moved(
            z=(me.z + 4) % N_Z,
            yh=jnp.where(self.outer, twin.yh, me.yh), yl=jnp.where(self.outer, twin.yl, me.yl),
        )

    def to_mirror(self):
        return remote(self.held.at[0], self.held.at[2], self.s1.at[0], self.r1.at[0], self.mirrored())

    def to_twin(self):
        return remote(self.held.at[0], self.held.at[1], self.s1.at[1], self.r1.at[1], self.twin)

    def copies(self, relayed, other):
        me = self.me
        if relayed:
            owner, at = self.mirrored(), 2
        elif other:
            owner = me.moved(
                yh=jnp.where(self.outer, self.twin.yh, me.yh),
                yl=jnp.where(self.outer, self.twin.yl, me.yl),
            )
            at = self.outer.astype(jnp.int32)
        else:
            owner, at = me, 0
        src = self.held.at[at]
        dst = self.slot(owner.z % 2, owner.yl, me.x)
        recv = self.r2.at[owner.z % 2, owner.yl, me.x]
        for i, dz in enumerate(self.STEPS):
            to = me.moved(
                x=owner.z // 2, yl=owner.yh, yh=1 - owner.yh if other else owner.yh,
                z=self.plane(me.z, dz),
            )
            copy = remote(src, dst, self.s2.at[relayed, other, i], recv, to)
            if dz == 0 and not other and not relayed:
                stays = jnp.logical_and(me.x == me.z // 2, self.outer)
                yield copy, pltpu.make_async_copy(src, dst, recv), stays
            else:
                yield copy, None, None

    def send(self, relayed, other):
        for copy, keep, stays in self.copies(relayed, other):
            if keep is None:
                copy.start()
            else:
                pl.when(stays)(keep.start)
                pl.when(jnp.logical_not(stays))(copy.start)

    def start(self):
        self.to_mirror().start()
        pl.when(self.outer)(self.to_twin().start)
        self.send(0, 0)
        pl.when(self.outer)(self.to_twin().wait_recv)
        self.send(0, 1)

    def relay(self):
        self.to_mirror().wait_recv()
        self.send(1, 1)
        self.send(1, 0)

    def away(self, source, c):
        dz = (self.me.z + N_Z - source) % N_Z
        return jnp.where(c == 0, dz, (N_Z - dz) % N_Z)

    @staticmethod
    def direct(away):
        return jnp.logical_or(away <= 2, away == N_Z - 1)

    def order(self, i, c):
        first = jnp.where(self.direct(self.away(2 * self.me.x, c)), 0, 1)
        return jnp.where(i < 2, first, 1 - first), i % 2

    def to_sibling(self, zz, yl):
        me = self.me
        rows = self.unit(zz, me.c, yl)
        return remote(rows, rows, self.s3.at[zz, yl], self.r3.at[zz, yl], me.moved(c=1 - me.c))

    def take_own(self, zz, yl):
        for x in range(N_X):
            arrived(self.slot(zz, yl, x), self.r2.at[zz, yl, x])
        self.to_sibling(zz, yl).start()

    def take_sibling(self, zz, yl):
        arrived(self.unit(zz, 1 - self.me.c, yl), self.r3.at[zz, yl])

    def finish(self):
        self.to_mirror().wait_send()
        pl.when(self.outer)(self.to_twin().wait_send)
        for relayed in range(2):
            for other in range(2):
                for copy, keep, stays in self.copies(relayed, other):
                    if keep is None:
                        copy.wait_send()
                    else:
                        pl.when(jnp.logical_not(stays))(copy.wait_send)
        for zz in range(2):
            for yl in range(N_Y):
                self.to_sibling(zz, yl).wait_send()

    def greet(self, greet):
        me = self.me
        greet(self.mirrored())
        pl.when(self.outer)(functools.partial(greet, self.twin))
        for zz in range(2):
            source = 2 * me.x + zz
            dz = self.away(source, me.c)
            direct = self.direct(dz)
            z = jnp.where(direct, source, (source + 4) % N_Z)
            near = jnp.logical_and(direct, self.outer)
            swap = jnp.where(near, 0, 1)
            for x in range(N_X):
                outer = me.moved(x=x, z=z, yl=(me.yl + swap) % 2, yh=(me.yl + swap) % 2)
                itself = jnp.logical_and(jnp.logical_and(x == me.x, z == me.z), near)
                pl.when(jnp.logical_not(itself))(functools.partial(greet, outer))
                greet(me.moved(x=x, z=z, yl=1 - me.yl, yh=me.yl))
        stays = jnp.logical_and(me.x == me.z // 2, self.outer)
        return 17 + self.outer.astype(jnp.int32) - stays.astype(jnp.int32)


def each_unit(spread, work):
    def take(p, n):
        own = jnp.logical_or(p < 2, jnp.logical_or(p == 3, p == 5))
        i = jnp.where(own, (p + 1) // 2, (p - 1) // 2)
        i = jnp.where(p == 7, 3, i)
        c = jnp.where(own, spread.me.c, 1 - spread.me.c)
        zz, yl = spread.order(i, c)
        pl.when(own)(lambda: spread.take_own(zz, yl))
        pl.when(jnp.logical_not(own))(lambda: spread.take_sibling(zz, yl))
        work(zz, c, yl, n)

    def step(p, carry):
        take(2 * p, 0)
        take(2 * p + 1, 1)
        return carry

    lax.fori_loop(0, 4, step, 0)


def kernel(
    live_ref, feat_ref, adj_ref, w_self_ref, w_neigh_ref, bias_ref, pos_ref, neg_ref,
    emb_ref, loss_ref,
    adj, w_self, w_neigh, bias, tables, live,
    held_f, full_f, acc, part, got, held_k, full_k, query, scaled_query, window, soft_0, soft_1, last, sums,
    losses, load_sem, store_sem, f1s, f1r, f2s, f2r, f3s, f3r, k1s, k1r, k2s, k2r, k3s, k3r, ps, pr, qs, qr,
):
    row, rep = lax.axis_index("row"), lax.axis_index("rep")
    me = Place(row // (N_Z * N_C), (row // N_C) % N_Z, row % N_C, rep // N_X, rep % N_X)
    block, channels = feat_ref.shape
    piece = block // N_REP
    lists = pos_ref.shape[2]
    own_rows = pl.ds(pl.multiple_of(rep * piece, 16), piece)
    loads = [
        pltpu.make_async_copy(src, dst, load_sem.at[i])
        for i, (src, dst) in enumerate((
            (feat_ref.at[own_rows, :], held_f.at[0]), (pos_ref, tables.at[0]), (neg_ref, tables.at[1]),
            (live_ref, live), (adj_ref, adj),
            (w_self_ref, w_self), (w_neigh_ref, w_neigh), (bias_ref, bias),
        ))
    ]
    loads[0].start()
    feats = Spread(me, piece, held_f, full_f, (f1s, f1r, f2s, f2r, f3s, f3r))
    keys = Spread(me, piece, held_k, full_k, (k1s, k1r, k2s, k2r, k3s, k3r))
    own = held_k.at[0]
    pending = []

    barrier = pltpu.get_barrier_semaphore()

    def greet(place):
        pl.semaphore_signal(barrier, inc=1, device_id=place.device, device_id_type=MESH)

    targets = feats.greet(greet)
    for d in range(1, N_REP):
        s = (rep + d) % N_REP
        greet(me.moved(yl=s // N_X, x=s % N_X))
    greet(me.moved(c=1 - me.c))
    for load in loads[1:]:
        load.start()
    loads[0].wait()
    pl.semaphore_wait(barrier, targets + (N_REP - 1) + 1)

    feats.start()

    for load in loads[1:3]:
        load.wait()
    half_block = N_X * piece
    row_at = lax.broadcasted_iota(jnp.int32, (TILE, lists), 0)
    nothing = jnp.zeros((half_block, lists), jnp.bfloat16)
    first = [tables[half, 1] * block + tables[half, 2] for half in range(2)]

    def fill(unit, carry):
        window[unit, :half_block, lists:] = nothing
        window[unit, half_block:, :lists] = nothing
        for half in range(2):
            for j in range(0, half_block, TILE):
                since = row_at + (unit * half_block + j) - first[half]
                inside = jnp.logical_and(since >= 0, since < TILE)
                at = half * half_block + j
                window[unit, at : at + TILE, half * lists : (half + 1) * lists] = jnp.where(
                    inside, 1.0, 0.0
                ).astype(jnp.bfloat16)
        return carry

    lax.fori_loop(0, 8, fill, 0)
    acc[...] = jnp.zeros_like(acc)
    sums[...] = jnp.zeros_like(sums)

    feats.relay()
    for load in loads[3:]:
        load.wait()

    def aggregate(zz, c, yl, n):
        k = zz * N_C + c
        flag = (live[0, k] > 0).astype(jnp.float32).astype(jnp.bfloat16)
        at = pl.ds(pl.multiple_of(k * block + yl * half_block, TILE), half_block)
        acc[...] += jnp.dot(
            adj[:, at], full_f[at, :] * flag, preferred_element_type=jnp.float32
        )

    each_unit(feats, aggregate)
    pending.append(feats.finish)

    part[...] = acc[...].astype(part.dtype)

    def partial_to(d):
        s = (rep + d) % N_REP
        return remote(
            part.at[pl.ds(pl.multiple_of(s * piece, 16), piece), :],
            got.at[d - 1], ps.at[d - 1], pr.at[d - 1], me.moved(yl=s // N_X, x=s % N_X),
        )

    for d in range(1, N_REP):
        partial_to(d).start()
    pending.extend(partial_to(d).wait_send for d in range(1, N_REP))
    projected = jnp.dot(held_f[0], w_self[...], preferred_element_type=jnp.float32)
    neighbour = acc[own_rows, :]
    for d in range(1, N_REP):
        partial_to(d).wait_recv()
        neighbour = neighbour + got[d - 1].astype(jnp.float32)
    projected = projected + jnp.dot(
        neighbour.astype(jnp.bfloat16), w_neigh[...], preferred_element_type=jnp.float32
    )
    projected = projected + bias[...]
    scaled = projected * lax.rsqrt(jnp.mean(projected * projected, axis=-1, keepdims=True) + 1e-06)
    held_k[0] = scaled.astype(jnp.bfloat16)

    def query_to(d):
        x = (me.x + d) % N_X
        return remote(own, query.at[own_rows, :], qs.at[d - 1], qr.at[d - 1], me.moved(x=x))

    def query_half(yl):
        rows = query.at[pl.ds(pl.multiple_of(yl * half_block, TILE), half_block), :]
        return remote(rows, rows, qs.at[N_X - 1], qr.at[N_X - 1], me.moved(yl=1 - me.yl))

    for d in range(1, N_X):
        query_to(d).start()
    keys.start()
    query[own_rows, :] = held_k[0]
    store_emb = pltpu.make_async_copy(own, emb_ref, store_sem.at[0])
    store_emb.start()
    pending.append(store_emb.wait)
    for d in range(1, N_X):
        query_to(d).wait_recv()
    query_half(me.yl).start()
    pending.extend(query_to(d).wait_send for d in range(1, N_X))
    pending.append(query_half(me.yl).wait_send)

    keys.relay()
    query_half(1 - me.yl).wait_recv()
    scaled_query[...] = query[...] * channels ** -0.5
    soft = (soft_0, soft_1)

    def add_windows(ref):
        sums[...] += jnp.dot(ref[...], window[last[0]], preferred_element_type=jnp.float32)

    def score(zz, c, yl, n):
        unit = (zz * N_C + c) * N_Y + yl
        add_windows(soft[1 - n])
        for j in range(0, half_block, TILE):
            at = pl.ds(pl.multiple_of(unit * half_block + j, TILE), TILE)
            t = lax.dot_general(
                scaled_query[...], full_k[at, :], (((1,), (1,)), ((), ())),
                preferred_element_type=jnp.float32,
            )
            low, high = jnp.minimum(t, 0.0), jnp.maximum(t, 0.0)
            e = jnp.exp(low - high)
            tail = jnp.where(e < 2.0 ** -12, e, jnp.log(1.0 + e))
            soft[n][:, j : j + TILE] = (tail - low).astype(jnp.bfloat16)
            soft[n][:, half_block + j : half_block + j + TILE] = (tail + high).astype(jnp.bfloat16)
        last[0] = unit

    soft_1[...] = jnp.zeros_like(soft_1)
    last[0] = 0
    each_unit(keys, score)
    add_windows(soft_1)
    pending.append(keys.finish)

    for half in range(2):
        loss = jnp.zeros((TILE, lists), jnp.float32)
        for q in range(block // TILE):
            tile = sums[q * TILE : (q + 1) * TILE, half * lists : (half + 1) * lists]
            loss = jnp.where(tables[half, 0] == q, tile, loss)
        losses[half] = jnp.transpose(loss * (1.0 / TILE))
    store_loss = pltpu.make_async_copy(losses, loss_ref, store_sem.at[1])
    store_loss.start()
    pending.append(store_loss.wait)
    for wait in pending:
        wait()


def hand_out(emb_in, loss_in, emb_ref, pos_ref, neg_ref):
    emb_ref[...] = emb_in[...]
    pos_ref[...] = loss_in[0]
    neg_ref[...] = loss_in[1]


def per_device(features, adjacency, tile_live, w_self, w_neigh, bias_vector, pos_pairs, neg_pairs):
    block, channels = features.shape
    sources = adjacency.shape[1]
    piece = block // N_REP
    lists = pos_pairs.shape[1]
    table = (pos_pairs.shape[2], 1, lists)
    place = pl.BlockSpec(memory_space=pl.ANY)
    vmem = pl.BlockSpec(memory_space=pltpu.VMEM)
    dma = pltpu.SemaphoreType.DMA
    spread_sems = [
        dma((2,)), dma((2,)), dma((2, 2, 4)), dma((2, N_Y, N_X)), dma((2, N_Y)), dma((2, N_Y)),
    ]
    bf16 = jnp.bfloat16
    f32 = jnp.float32
    limit = 60 * 1024 * 1024
    embedding, losses = pl.pallas_call(
        kernel,
        out_shape=(
            jax.ShapeDtypeStruct((piece, channels), bf16),
            jax.ShapeDtypeStruct((2, lists, TILE), f32),
        ),
        in_specs=[place] * 8,
        out_specs=(place,) * 2,
        scratch_shapes=[
            pltpu.VMEM((block, sources), bf16),
            pltpu.VMEM((channels, channels), bf16),
            pltpu.VMEM((channels, channels), bf16),
            pltpu.VMEM((1, channels), f32),
            pltpu.VMEM((2, *table), jnp.int32),
            pltpu.SMEM((1, 4), jnp.int32),
            pltpu.VMEM((3, piece, channels), bf16),
            pltpu.VMEM((sources, channels), bf16),
            pltpu.VMEM((block, channels), f32),
            pltpu.VMEM((block, channels), PART_TYPE),
            pltpu.VMEM((N_REP - 1, piece, channels), PART_TYPE),
            pltpu.VMEM((3, piece, channels), bf16),
            pltpu.VMEM((sources, channels), bf16),
            pltpu.VMEM((block, channels), bf16),
            pltpu.VMEM((block, channels), bf16),
            pltpu.VMEM((8, block, 2 * lists), bf16),
            pltpu.VMEM((block, block), bf16),
            pltpu.VMEM((block, block), bf16),
            pltpu.SMEM((1,), jnp.int32),
            pltpu.VMEM((block, 2 * lists), f32),
            pltpu.VMEM((2, lists, TILE), f32),
            dma((8,)), dma((2,)),
            *spread_sems,
            *spread_sems,
            dma((N_REP - 1,)), dma((N_REP - 1,)), dma((N_X,)), dma((N_X,)),
        ],
        compiler_params=pltpu.CompilerParams(
            collective_id=0, has_side_effects=True, vmem_limit_bytes=limit
        ),
    )(
        tile_live, features, adjacency, w_self, w_neigh, bias_vector.reshape(1, channels),
        pos_pairs.transpose(2, 0, 1), neg_pairs.transpose(2, 0, 1),
    )
    embedding, pos_loss, neg_loss = pl.pallas_call(
        hand_out,
        out_shape=(
            jax.ShapeDtypeStruct((piece, channels), bf16),
            jax.ShapeDtypeStruct((lists, TILE), f32),
            jax.ShapeDtypeStruct((lists, TILE), f32),
        ),
        in_specs=[vmem] * 2,
        out_specs=(vmem,) * 3,
        compiler_params=pltpu.CompilerParams(vmem_limit_bytes=limit),
    )(embedding, losses)
    return embedding, pos_loss[None], neg_loss[None]


def solution(mesh):
    return jax.shard_map(
        per_device,
        mesh=mesh,
        in_specs=(
            P("row", None),
            P("row", "rep"),
            P("row", "rep"),
            P(),
            P(),
            P(),
            P("row", "rep", None),
            P("row", "rep", None),
        ),
        out_specs=(P(("row", "rep"), None), P("row", "rep", None), P("row", "rep", None)),
        check_vma=False,
    )
```

time: 77.4 us -> 65.8 us (0.85)
  the two profiles are of different devices: /device:TPU:32 before, /device:TPU:36 now
where the time goes in v3:
time: 65.8 us; the launch traced here: 65.3 us
  Pallas kernels  64.7 us (98%)
    pallas_call x1, Pallas kernels, per_device(): pl.pallas_call(kernel, out_shape=(jax.ShapeDtypeStruct((piece, channels),...  63 us
    pallas_call x1, Pallas kernels, per_device(): pl.pallas_call(hand_out, out_shape=(jax.ShapeDtypeStruct((piece, channels...  1.61 us

profile of v3, /device:TPU:36, one launch (start us, length us, event | category | flops | bytes accessed | tf_op | source)
XLA Modules:
  0.0 65.3 jit_solution(9274418922358228258)
XLA Ops:
  0.6 63.0 %shard_map.103 = (bf16[96,256]{1,0:T(8,128)(2,1)}, f32[2,128,128]{2,1,0:T(8,128)}) custom-call(s32[1,4]{1,0:T(1,128)} %live_ref.1, bf16[768,256]{1,0:T(8,128)(2,1)} %feat_ref.1, bf16[768,3072]{1,0:T(8,128)(2,1)} %adj_ref.1, bf16[256,256]{1,0:T(8,128)(2,1)} %w_self_ref.1, bf16[256,256]{1,0:T(8,128)(2,1)} %w_neigh_ref.1, f32[1,256]{1,0:T(1,128)} %bitcast.7, ...), custom_call_target="tpu_custom_call" | custom-call | tf_op jit(solution)/shard_map/pallas_call | solution.py:396
  63.7 1.6 %shard_map.104 = (bf16[96,256]{1,0:T(8,128)(2,1)}, f32[128,128]{1,0:T(8,128)}, f32[128,128]{1,0:T(8,128)}) custom-call(bf16[96,256]{1,0:T(8,128)(2,1)} %get-tuple-element.8.emb_in, f32[2,128,128]{2,1,0:T(8,128)} %get-tuple-element.9.loss_in), custom_call_target="tpu_custom_call" | custom-call | tf_op jit(solution)/shard_map/pallas_call | solution.py:438

commit v4 on v3

--- a/solution.py
+++ b/solution.py
@@ -14,6 +14,14 @@
 PART_TYPE = jnp.bfloat16
 
 
+def mod(a, n):
+    return lax.rem(a, jnp.int32(n))
+
+
+def div(a, n):
+    return lax.div(a, jnp.int32(n))
+
+
 class Place:
     def __init__(self, yh, z, c, yl, x):
         self.yh, self.z, self.c, self.yl, self.x = yh, z, c, yl, x
@@ -43,13 +51,26 @@
 
 
 class Spread:
-    STEPS = (2, 1, -1, 0)
+    SHIFTS = (0, 3, -3)
+    STEPS = ((1, -1, 0), (1, -1, 0), (1, 0))
 
     def __init__(self, me, piece, held, full, sems):
         self.me, self.piece, self.held, self.full = me, piece, held, full
         self.s1, self.r1, self.s2, self.r2, self.s3, self.r3 = sems
         self.outer = me.yl == me.yh
         self.twin = me.moved(yh=1 - me.yh, yl=1 - me.yl)
+        way = 1 - 2 * me.c
+        self.planes = {dz: mod(me.z + N_Z + dz * way, N_Z) for dz in (0, 1, -1, 3, -3)}
+        self.side = dict(
+            yh=jnp.where(self.outer, self.twin.yh, me.yh), yl=jnp.where(self.outer, self.twin.yl, me.yl)
+        )
+        away = mod(me.z + N_Z - 2 * me.x, N_Z)
+        first = [
+            jnp.where(self.direct(a), 0, 1) for a in (away, mod(N_Z - away, N_Z))
+        ]
+        self.first = (
+            jnp.where(me.c == 0, first[0], first[1]), jnp.where(me.c == 0, first[1], first[0])
+        )
 
     def unit(self, zz, c, yl):
         rows = N_X * self.piece
@@ -60,80 +81,77 @@
         at = (((zz * N_C + self.me.c) * N_Y + yl) * N_X + x) * self.piece
         return self.full.at[pl.ds(pl.multiple_of(at, 16), self.piece), :]
 
-    def plane(self, source, dz):
-        return (source + N_Z + dz * (1 - 2 * self.me.c)) % N_Z
-
-    def mirrored(self):
-        me, twin = self.me, self.twin
-        return me.moved(
-            z=(me.z + 4) % N_Z,
-            yh=jnp.where(self.outer, twin.yh, me.yh), yl=jnp.where(self.outer, twin.yl, me.yl),
+    def beside(self, dz):
+        return self.me.moved(z=self.planes[dz], **self.side)
+
+    def to_holder(self, k):
+        return remote(
+            self.held.at[0], self.held.at[1 + k], self.s1.at[k], self.r1.at[k],
+            self.beside(self.SHIFTS[k]),
         )
 
-    def to_mirror(self):
-        return remote(self.held.at[0], self.held.at[2], self.s1.at[0], self.r1.at[0], self.mirrored())
-
     def to_twin(self):
-        return remote(self.held.at[0], self.held.at[1], self.s1.at[1], self.r1.at[1], self.twin)
-
-    def copies(self, relayed, other):
+        return remote(self.held.at[0], self.held.at[1], self.s1.at[0], self.r1.at[0], self.twin)
+
+    def copies(self, k, other):
         me = self.me
-        if relayed:
-            owner, at = self.mirrored(), 2
+        if k:
+            owner, at = self.beside(-self.SHIFTS[k]), 1 + k
         elif other:
-            owner = me.moved(
-                yh=jnp.where(self.outer, self.twin.yh, me.yh),
-                yl=jnp.where(self.outer, self.twin.yl, me.yl),
-            )
-            at = self.outer.astype(jnp.int32)
+            owner, at = self.beside(0), jnp.where(self.outer, 1, 0)
         else:
             owner, at = me, 0
         src = self.held.at[at]
-        dst = self.slot(owner.z % 2, owner.yl, me.x)
-        recv = self.r2.at[owner.z % 2, owner.yl, me.x]
-        for i, dz in enumerate(self.STEPS):
+        zz, x = mod(owner.z, 2), div(owner.z, 2)
+        dst = self.slot(zz, owner.yl, me.x)
+        recv = self.r2.at[zz, owner.yl, me.x]
+        for i, dz in enumerate(self.STEPS[k]):
             to = me.moved(
-                x=owner.z // 2, yl=owner.yh, yh=1 - owner.yh if other else owner.yh,
-                z=self.plane(me.z, dz),
+                x=x, yl=owner.yh, yh=1 - owner.yh if other else owner.yh,
+                z=self.planes[dz],
             )
-            copy = remote(src, dst, self.s2.at[relayed, other, i], recv, to)
-            if dz == 0 and not other and not relayed:
-                stays = jnp.logical_and(me.x == me.z // 2, self.outer)
+            copy = remote(src, dst, self.s2.at[k, other, i], recv, to)
+            if dz == 0 and not other and not k:
+                stays = jnp.logical_and(me.x == x, self.outer)
                 yield copy, pltpu.make_async_copy(src, dst, recv), stays
             else:
                 yield copy, None, None
 
-    def send(self, relayed, other):
-        for copy, keep, stays in self.copies(relayed, other):
+    def send(self, k, other):
+        for copy, keep, stays in self.copies(k, other):
             if keep is None:
                 copy.start()
             else:
                 pl.when(stays)(keep.start)
                 pl.when(jnp.logical_not(stays))(copy.start)
 
+    def start_holders(self):
+        self.to_holder(1).start()
+        self.to_holder(2).start()
+        pl.when(self.outer)(self.to_twin().start)
+
     def start(self):
-        self.to_mirror().start()
-        pl.when(self.outer)(self.to_twin().start)
         self.send(0, 0)
         pl.when(self.outer)(self.to_twin().wait_recv)
         self.send(0, 1)
 
     def relay(self):
-        self.to_mirror().wait_recv()
-        self.send(1, 1)
-        self.send(1, 0)
+        for k in (1, 2):
+            self.to_holder(k).wait_recv()
+            self.send(k, 1)
+            self.send(k, 0)
 
     def away(self, source, c):
-        dz = (self.me.z + N_Z - source) % N_Z
-        return jnp.where(c == 0, dz, (N_Z - dz) % N_Z)
+        dz = mod(self.me.z + N_Z - source, N_Z)
+        return jnp.where(c == 0, dz, mod(N_Z - dz, N_Z))
 
     @staticmethod
     def direct(away):
-        return jnp.logical_or(away <= 2, away == N_Z - 1)
-
-    def order(self, i, c):
-        first = jnp.where(self.direct(self.away(2 * self.me.x, c)), 0, 1)
-        return jnp.where(i < 2, first, 1 - first), i % 2
+        return jnp.logical_or(away <= 1, away == N_Z - 1)
+
+    def order(self, i, sibling):
+        first = self.first[sibling]
+        return jnp.where(i == 0, first, 1 - first)
 
     def to_sibling(self, zz, yl):
         me = self.me
@@ -149,11 +167,12 @@
         arrived(self.unit(zz, 1 - self.me.c, yl), self.r3.at[zz, yl])
 
     def finish(self):
-        self.to_mirror().wait_send()
+        self.to_holder(1).wait_send()
+        self.to_holder(2).wait_send()
         pl.when(self.outer)(self.to_twin().wait_send)
-        for relayed in range(2):
+        for k in range(3):
             for other in range(2):
-                for copy, keep, stays in self.copies(relayed, other):
+                for copy, keep, stays in self.copies(k, other):
                     if keep is None:
                         copy.wait_send()
                     else:
@@ -164,13 +183,15 @@
 
     def greet(self, greet):
         me = self.me
-        greet(self.mirrored())
+        greet(self.beside(3))
+        greet(self.beside(-3))
         pl.when(self.outer)(functools.partial(greet, self.twin))
         for zz in range(2):
             source = 2 * me.x + zz
-            dz = self.away(source, me.c)
-            direct = self.direct(dz)
-            z = jnp.where(direct, source, (source + 4) % N_Z)
+            away = self.away(source, me.c)
+            direct = self.direct(away)
+            shift = jnp.where(direct, 0, jnp.where(away <= 4, 3, N_Z - 3))
+            z = mod(source + jnp.where(me.c == 0, shift, N_Z - shift), N_Z)
             near = jnp.logical_and(direct, self.outer)
             swap = jnp.where(near, 0, 1)
             for x in range(N_X):
@@ -178,27 +199,31 @@
                 itself = jnp.logical_and(jnp.logical_and(x == me.x, z == me.z), near)
                 pl.when(jnp.logical_not(itself))(functools.partial(greet, outer))
                 greet(me.moved(x=x, z=z, yl=1 - me.yl, yh=me.yl))
-        stays = jnp.logical_and(me.x == me.z // 2, self.outer)
-        return 17 + self.outer.astype(jnp.int32) - stays.astype(jnp.int32)
-
-
-def each_unit(spread, work):
-    def take(p, n):
-        own = jnp.logical_or(p < 2, jnp.logical_or(p == 3, p == 5))
-        i = jnp.where(own, (p + 1) // 2, (p - 1) // 2)
-        i = jnp.where(p == 7, 3, i)
-        c = jnp.where(own, spread.me.c, 1 - spread.me.c)
-        zz, yl = spread.order(i, c)
-        pl.when(own)(lambda: spread.take_own(zz, yl))
-        pl.when(jnp.logical_not(own))(lambda: spread.take_sibling(zz, yl))
-        work(zz, c, yl, n)
-
-    def step(p, carry):
-        take(2 * p, 0)
-        take(2 * p + 1, 1)
+        stays = jnp.logical_and(me.x == div(me.z, 2), self.outer)
+        return 18 + jnp.where(self.outer, 1, 0) - jnp.where(stays, 1, 0)
+
+
+def each_block(spread, work):
+    me = spread.me
+
+    def take_own(i):
+        zz = spread.order(i, 0)
+        for yl in range(N_Y):
+            spread.take_own(zz, yl)
+        return zz, me.c
+
+    def take_sibling(i):
+        zz = spread.order(i, 1)
+        for yl in range(N_Y):
+            spread.take_sibling(zz, yl)
+        return zz, 1 - me.c
+
+    def step(q, carry):
+        for n in range(2):
+            work(*lax.cond(q == 0, take_own, take_sibling, n), n)
         return carry
 
-    lax.fori_loop(0, 4, step, 0)
+    lax.fori_loop(0, 2, step, 0)
 
 
 def kernel(
@@ -209,7 +234,11 @@
     losses, load_sem, store_sem, f1s, f1r, f2s, f2r, f3s, f3r, k1s, k1r, k2s, k2r, k3s, k3r, ps, pr, qs, qr,
 ):
     row, rep = lax.axis_index("row"), lax.axis_index("rep")
-    me = Place(row // (N_Z * N_C), (row // N_C) % N_Z, row % N_C, rep // N_X, rep % N_X)
+    me = Place(div(row, N_Z * N_C), mod(div(row, N_C), N_Z), mod(row, N_C), div(rep, N_X), mod(rep, N_X))
+    peers = [
+        me.moved(yl=1 - me.yl if dy else me.yl, x=mod(me.x + dx, N_X))
+        for dy, dx in ((1, 2), (1, 1), (1, 3), (0, 2), (0, 1), (0, 3), (1, 0))
+    ]
     block, channels = feat_ref.shape
     piece = block // N_REP
     lists = pos_ref.shape[2]
@@ -234,38 +263,38 @@
         pl.semaphore_signal(barrier, inc=1, device_id=place.device, device_id_type=MESH)
 
     targets = feats.greet(greet)
-    for d in range(1, N_REP):
-        s = (rep + d) % N_REP
-        greet(me.moved(yl=s // N_X, x=s % N_X))
+    for peer in peers:
+        greet(peer)
     greet(me.moved(c=1 - me.c))
     for load in loads[1:]:
         load.start()
     loads[0].wait()
     pl.semaphore_wait(barrier, targets + (N_REP - 1) + 1)
 
+    feats.start_holders()
     feats.start()
 
     for load in loads[1:3]:
         load.wait()
     half_block = N_X * piece
     row_at = lax.broadcasted_iota(jnp.int32, (TILE, lists), 0)
-    nothing = jnp.zeros((half_block, lists), jnp.bfloat16)
+    nothing = jnp.zeros((block, lists), jnp.bfloat16)
     first = [tables[half, 1] * block + tables[half, 2] for half in range(2)]
 
-    def fill(unit, carry):
-        window[unit, :half_block, lists:] = nothing
-        window[unit, half_block:, :lists] = nothing
+    def fill(k, carry):
+        window[k, :block, lists:] = nothing
+        window[k, block:, :lists] = nothing
         for half in range(2):
-            for j in range(0, half_block, TILE):
-                since = row_at + (unit * half_block + j) - first[half]
+            for j in range(0, block, TILE):
+                since = row_at + (k * block + j) - first[half]
                 inside = jnp.logical_and(since >= 0, since < TILE)
-                at = half * half_block + j
-                window[unit, at : at + TILE, half * lists : (half + 1) * lists] = jnp.where(
+                at = half * block + j
+                window[k, at : at + TILE, half * lists : (half + 1) * lists] = jnp.where(
                     inside, 1.0, 0.0
                 ).astype(jnp.bfloat16)
         return carry
 
-    lax.fori_loop(0, 8, fill, 0)
+    lax.fori_loop(0, 4, fill, 0)
     acc[...] = jnp.zeros_like(acc)
     sums[...] = jnp.zeros_like(sums)
 
@@ -273,34 +302,34 @@
     for load in loads[3:]:
         load.wait()
 
-    def aggregate(zz, c, yl, n):
+    def aggregate(zz, c, n):
         k = zz * N_C + c
         flag = (live[0, k] > 0).astype(jnp.float32).astype(jnp.bfloat16)
-        at = pl.ds(pl.multiple_of(k * block + yl * half_block, TILE), half_block)
+        at = pl.ds(pl.multiple_of(k * block, TILE), block)
         acc[...] += jnp.dot(
             adj[:, at], full_f[at, :] * flag, preferred_element_type=jnp.float32
         )
 
-    each_unit(feats, aggregate)
+    each_block(feats, aggregate)
     pending.append(feats.finish)
 
     part[...] = acc[...].astype(part.dtype)
 
     def partial_to(d):
-        s = (rep + d) % N_REP
+        at = (peers[d].yl * N_X + peers[d].x) * piece
         return remote(
-            part.at[pl.ds(pl.multiple_of(s * piece, 16), piece), :],
-            got.at[d - 1], ps.at[d - 1], pr.at[d - 1], me.moved(yl=s // N_X, x=s % N_X),
+            part.at[pl.ds(pl.multiple_of(at, 16), piece), :],
+            got.at[d], ps.at[d], pr.at[d], peers[d],
         )
 
-    for d in range(1, N_REP):
+    for d in range(N_REP - 1):
         partial_to(d).start()
-    pending.extend(partial_to(d).wait_send for d in range(1, N_REP))
+    pending.extend(partial_to(d).wait_send for d in range(N_REP - 1))
     projected = jnp.dot(held_f[0], w_self[...], preferred_element_type=jnp.float32)
     neighbour = acc[own_rows, :]
-    for d in range(1, N_REP):
+    for d in range(N_REP - 1):
         partial_to(d).wait_recv()
-        neighbour = neighbour + got[d - 1].astype(jnp.float32)
+        neighbour = neighbour + got[d].astype(jnp.float32)
     projected = projected + jnp.dot(
         neighbour.astype(jnp.bfloat16), w_neigh[...], preferred_element_type=jnp.float32
     )
@@ -309,19 +338,23 @@
     held_k[0] = scaled.astype(jnp.bfloat16)
 
     def query_to(d):
-        x = (me.x + d) % N_X
+        x = mod(me.x + d, N_X)
         return remote(own, query.at[own_rows, :], qs.at[d - 1], qr.at[d - 1], me.moved(x=x))
 
     def query_half(yl):
         rows = query.at[pl.ds(pl.multiple_of(yl * half_block, TILE), half_block), :]
         return remote(rows, rows, qs.at[N_X - 1], qr.at[N_X - 1], me.moved(yl=1 - me.yl))
 
+    keys.start_holders()
     for d in range(1, N_X):
         query_to(d).start()
     keys.start()
     query[own_rows, :] = held_k[0]
     store_emb = pltpu.make_async_copy(own, emb_ref, store_sem.at[0])
     store_emb.start()
+    for wait in pending:
+        wait()
+    pending.clear()
     pending.append(store_emb.wait)
     for d in range(1, N_X):
         query_to(d).wait_recv()
@@ -337,11 +370,11 @@
     def add_windows(ref):
         sums[...] += jnp.dot(ref[...], window[last[0]], preferred_element_type=jnp.float32)
 
-    def score(zz, c, yl, n):
-        unit = (zz * N_C + c) * N_Y + yl
+    def score(zz, c, n):
+        k = zz * N_C + c
         add_windows(soft[1 - n])
-        for j in range(0, half_block, TILE):
-            at = pl.ds(pl.multiple_of(unit * half_block + j, TILE), TILE)
+        for j in range(0, block, TILE):
+            at = pl.ds(pl.multiple_of(k * block + j, TILE), TILE)
             t = lax.dot_general(
                 scaled_query[...], full_k[at, :], (((1,), (1,)), ((), ())),
                 preferred_element_type=jnp.float32,
@@ -350,12 +383,12 @@
             e = jnp.exp(low - high)
             tail = jnp.where(e < 2.0 ** -12, e, jnp.log(1.0 + e))
             soft[n][:, j : j + TILE] = (tail - low).astype(jnp.bfloat16)
-            soft[n][:, half_block + j : half_block + j + TILE] = (tail + high).astype(jnp.bfloat16)
-        last[0] = unit
+            soft[n][:, block + j : block + j + TILE] = (tail + high).astype(jnp.bfloat16)
+        last[0] = k
 
     soft_1[...] = jnp.zeros_like(soft_1)
     last[0] = 0
-    each_unit(keys, score)
+    each_block(keys, score)
     add_windows(soft_1)
     pending.append(keys.finish)
 
@@ -388,7 +421,7 @@
     vmem = pl.BlockSpec(memory_space=pltpu.VMEM)
     dma = pltpu.SemaphoreType.DMA
     spread_sems = [
-        dma((2,)), dma((2,)), dma((2, 2, 4)), dma((2, N_Y, N_X)), dma((2, N_Y)), dma((2, N_Y)),
+        dma((3,)), dma((3,)), dma((3, 2, 3)), dma((2, N_Y, N_X)), dma((2, N_Y)), dma((2, N_Y)),
     ]
     bf16 = jnp.bfloat16
     f32 = jnp.float32
@@ -408,18 +441,18 @@
             pltpu.VMEM((1, channels), f32),
             pltpu.VMEM((2, *table), jnp.int32),
             pltpu.SMEM((1, 4), jnp.int32),
-            pltpu.VMEM((3, piece, channels), bf16),
+            pltpu.VMEM((4, piece, channels), bf16),
             pltpu.VMEM((sources, channels), bf16),
             pltpu.VMEM((block, channels), f32),
             pltpu.VMEM((block, channels), PART_TYPE),
             pltpu.VMEM((N_REP - 1, piece, channels), PART_TYPE),
-            pltpu.VMEM((3, piece, channels), bf16),
+            pltpu.VMEM((4, piece, channels), bf16),
             pltpu.VMEM((sources, channels), bf16),
             pltpu.VMEM((block, channels), bf16),
             pltpu.VMEM((block, channels), bf16),
-            pltpu.VMEM((8, block, 2 * lists), bf16),
-            pltpu.VMEM((block, block), bf16),
-            pltpu.VMEM((block, block), bf16),
+            pltpu.VMEM((4, 2 * block, 2 * lists), bf16),
+            pltpu.VMEM((block, 2 * block), bf16),
+            pltpu.VMEM((block, 2 * block), bf16),
             pltpu.SMEM((1,), jnp.int32),
             pltpu.VMEM((block, 2 * lists), f32),
             pltpu.VMEM((2, lists, TILE), f32),

time: 65.8 us -> 65.1 us (0.989)
  the two profiles are of different devices: /device:TPU:36 before, /device:TPU:2 now
where the time goes in v4:
time: 65.1 us; the launch traced here: 65 us
  Pallas kernels  64.3 us (99%)
    pallas_call x1, Pallas kernels, per_device(): pl.pallas_call(kernel, out_shape=(jax.ShapeDtypeStruct((piece, channels),...  62.7 us
    pallas_call x1, Pallas kernels, per_device(): pl.pallas_call(hand_out, out_shape=(jax.ShapeDtypeStruct((piece, channels...  1.61 us

profile of v4, /device:TPU:2, one launch (start us, length us, event | category | flops | bytes accessed | tf_op | source)
XLA Modules:
  0.0 65.0 jit_solution(9204429953984739805)
XLA Ops:
  0.6 62.7 %shard_map.103 = (bf16[96,256]{1,0:T(8,128)(2,1)}, f32[2,128,128]{2,1,0:T(8,128)}) custom-call(s32[1,4]{1,0:T(1,128)} %live_ref.1, bf16[768,256]{1,0:T(8,128)(2,1)} %feat_ref.1, bf16[768,3072]{1,0:T(8,128)(2,1)} %adj_ref.1, bf16[256,256]{1,0:T(8,128)(2,1)} %w_self_ref.1, bf16[256,256]{1,0:T(8,128)(2,1)} %w_neigh_ref.1, f32[1,256]{1,0:T(1,128)} %bitcast.7, ...), custom_call_target="tpu_custom_call" | custom-call | tf_op jit(solution)/shard_map/pallas_call | solution.py:429
  63.3 1.6 %shard_map.104 = (bf16[96,256]{1,0:T(8,128)(2,1)}, f32[128,128]{1,0:T(8,128)}, f32[128,128]{1,0:T(8,128)}) custom-call(bf16[96,256]{1,0:T(8,128)(2,1)} %get-tuple-element.8.emb_in, f32[2,128,128]{2,1,0:T(8,128)} %get-tuple-element.9.loss_in), custom_call_target="tpu_custom_call" | custom-call | tf_op jit(solution)/shard_map/pallas_call | solution.py:471

commit v5 on v4

--- a/solution.py
+++ b/solution.py
@@ -313,7 +313,6 @@
     each_block(feats, aggregate)
     pending.append(feats.finish)
 
-    part[...] = acc[...].astype(part.dtype)
 
     def partial_to(d):
         at = (peers[d].yl * N_X + peers[d].x) * piece
@@ -323,6 +322,8 @@
         )
 
     for d in range(N_REP - 1):
+        rows = pl.ds(pl.multiple_of((peers[d].yl * N_X + peers[d].x) * piece, 16), piece)
+        part[rows, :] = acc[rows, :].astype(part.dtype)
         partial_to(d).start()
     pending.extend(partial_to(d).wait_send for d in range(N_REP - 1))
     projected = jnp.dot(held_f[0], w_self[...], preferred_element_type=jnp.float32)

time: 65.1 us -> 66.9 us (1.028)
  the two profiles are of different devices: /device:TPU:2 before, /device:TPU:38 now
where the time goes in v5:
time: 66.9 us; the launch traced here: 66.7 us
  Pallas kernels  66.1 us (99%)
    pallas_call x1, Pallas kernels, per_device(): pl.pallas_call(kernel, out_shape=(jax.ShapeDtypeStruct((piece, channels),...  64.5 us
    pallas_call x1, Pallas kernels, per_device(): pl.pallas_call(hand_out, out_shape=(jax.ShapeDtypeStruct((piece, channels...  1.61 us

profile of v5, /device:TPU:38, one launch (start us, length us, event | category | flops | bytes accessed | tf_op | source)
XLA Modules:
  0.0 66.7 jit_solution(11469004003396395940)
XLA Ops:
  0.6 64.5 %shard_map.103 = (bf16[96,256]{1,0:T(8,128)(2,1)}, f32[2,128,128]{2,1,0:T(8,128)}) custom-call(s32[1,4]{1,0:T(1,128)} %live_ref.1, bf16[768,256]{1,0:T(8,128)(2,1)} %feat_ref.1, bf16[768,3072]{1,0:T(8,128)(2,1)} %adj_ref.1, bf16[256,256]{1,0:T(8,128)(2,1)} %w_self_ref.1, bf16[256,256]{1,0:T(8,128)(2,1)} %w_neigh_ref.1, f32[1,256]{1,0:T(1,128)} %bitcast.7, ...), custom_call_target="tpu_custom_call" | custom-call | tf_op jit(solution)/shard_map/pallas_call | solution.py:430
  65.1 1.6 %shard_map.104 = (bf16[96,256]{1,0:T(8,128)(2,1)}, f32[128,128]{1,0:T(8,128)}, f32[128,128]{1,0:T(8,128)}) custom-call(bf16[96,256]{1,0:T(8,128)(2,1)} %get-tuple-element.8.emb_in, f32[2,128,128]{2,1,0:T(8,128)} %get-tuple-element.9.loss_in), custom_call_target="tpu_custom_call" | custom-call | tf_op jit(solution)/shard_map/pallas_call | solution.py:472
